TPU v7x, 128 devices: a whole 4x4x4 slice. The times are simulated.
128 devices in a mesh: row: 8 (over x_lo, y), col: 16 (over z, x_hi, core).
Axes of the slice: x: 4 (x_hi: 2, x_lo: 2; x = x_hi * 2 + x_lo), y: 4, z: 4, core: 2. Of those that a mesh axis runs over, the one named last changes fastest.
Arguments:
- slab: float32 [4096, 4, 2048], P(('row', 'col')), may hold values from -0.75 to 0.75
- occ_energy: float32 [4], replicated, may hold values from -1.2 to -0.4
- vir_energy: float32 [2048], replicated, may hold values from 0.3 to 3.4
Outputs:
- amplitudes: float32 [6, 2048, 2048], P(None, 'row', 'col')
- pair_energy: float32 [6], replicated
All inputs are finite; a program needn't handle non-finite values.
Results may differ from a plain program's by a relative error of at most 0.0001.
Values sent between devices are 32-bit elements; how exact they have to be, the bound alone decides.
A program may use at most 128 MiB of HBM per device.

v0:
```python
import jax
import jax.numpy as jnp
from jax import lax
from jax.sharding import PartitionSpec as P

pair_list = [(0, 1), (0, 2), (0, 3), (1, 2), (1, 3), (2, 3)]


def contract(left, right):
    return jnp.einsum(
        "qia,qjb->iajb",
        left,
        right,
        precision=lax.Precision.HIGHEST,
        preferred_element_type=jnp.float32,
    )


def local(slab, occ_energy, vir_energy):
    per_dev, occ, nvir = slab.shape
    n_row = lax.axis_size("row")
    n_col = lax.axis_size("col")
    wide_a = nvir // n_row
    wide_b = nvir // n_col
    moved = lax.all_to_all(slab, "col", split_axis=2, concat_axis=0, tiled=True)
    stacked = lax.all_gather(moved, "row", axis=0, tiled=True)
    right_ops = (
        stacked.reshape(n_row, n_col, per_dev, occ, wide_b)
        .transpose(1, 0, 2, 3, 4)
        .reshape(n_row * n_col * per_dev, occ, wide_b)
    )
    left_part = lax.all_to_all(slab, "row", split_axis=2, concat_axis=0, tiled=True)
    left_ops = lax.all_gather(left_part, "col", axis=0, tiled=True)
    integrals = contract(left_ops, right_ops)
    energy_a = lax.dynamic_slice_in_dim(vir_energy, lax.axis_index("row") * wide_a, wide_a, 0)
    energy_b = lax.dynamic_slice_in_dim(vir_energy, lax.axis_index("col") * wide_b, wide_b, 0)
    amps = []
    shares = []
    for first, second in pair_list:
        direct = integrals[first, :, second, :]
        swapped = integrals[second, :, first, :]
        denom = occ_energy[first] + occ_energy[second] - energy_a[:, None] - energy_b[None, :]
        amp = direct / denom
        amps.append(amp)
        shares.append(jnp.sum(amp * (2.0 * direct - swapped)))
    total = lax.psum(jnp.stack(shares), ("row", "col"))
    return (jnp.stack(amps), 2.0 * total / (nvir * nvir))


def solution(mesh):
    return jax.shard_map(
        local,
        mesh=mesh,
        in_specs=(P(("row", "col"), None, None), P(), P()),
        out_specs=(P(None, "row", "col"), P()),
        check_vma=False,
    )
```

profile of v0, /device:TPU:1, one launch (start us, length us, event | category | flops | bytes accessed | tf_op | source)
XLA Modules:
  0.0 382.0 jit_solution(6284440146230831183)
XLA Ops:
  7.2 0.0 all-gather.5.cloned.1.call-start
  7.2 4.6 %copy.22 = f32[32,4,2048]{0,1,2:T(4,128)} copy(f32[32,4,2048]{2,1,0:T(4,128)} %param.3) | data formatting | bytes 2097152 | tf_op args[0]
  11.8 4.4 %reshape.334 = f32[16,1,16384]{2,1,0:T(1,128)S(1)} reshape(f32[2048,4,32]{2,1,0:T(4,128)} %bitcast.152) | data formatting | bytes 2097152
  16.2 26.0 %all_to_all.36 = f32[16,1,16384]{2,1,0:T(1,128)S(1)} all-to-all(f32[16,1,16384]{2,1,0:T(1,128)S(1)} %reshape.334), channel_id=1, replica_groups=mesh['row'=8,'col'=16] {'col'}, dimensions={0} | all-to-all | bytes 2097152 | tf_op jit(solution)/shard_map/all_to_all | solution.py:25
  42.2 0.5 broadcast.248
  42.7 3.1 reduce
  45.8 3.5 reshape.335
  49.4 4.6 %copy.34 = f32[32,4,16,128]{3,0,2,1:T(8,128)} copy(f32[32,4,16,128]{0,1,3,2:T(4,128)} %bitcast.154) | data formatting | bytes 2097152 | tf_op jit(solution)/shard_map/all_to_all | solution.py:25
  54.0 0.0 all-gather.3.cloned.1.call-start
  54.0 4.6 %reshape.336 = f32[8,1,32768]{2,1,0:T(1,128)S(1)} reshape(f32[2048,4,32]{2,1,0:T(4,128)} %bitcast.153) | data formatting | bytes 2097152
  58.6 32.3 %all_to_all.37 = f32[8,1,32768]{2,1,0:T(1,128)S(1)} all-to-all(f32[8,1,32768]{2,1,0:T(1,128)S(1)} %reshape.336), channel_id=1, replica_groups=mesh['row'=8,'col'=16] {'row'}, dimensions={0} | all-to-all | bytes 2097152 | tf_op jit(solution)/shard_map/all_to_all | solution.py:32
  90.9 3.1 reduce.1
  94.0 4.1 %reshape.337 = f32[2048,4,32]{2,1,0:T(4,128)} reshape(f32[8,32768]{1,0:T(8,128)S(1)} %reduce.1) | data formatting | bytes 2097152
  98.1 3.5 copy.32
  101.6 1.3 copy.25
  103.0 0.7 fusion.26
  111.5 0.8 dynamic_slice.7
  112.3 0.8 broadcast_subtract_fusion
  113.0 41.6 %all-gather.5.cloned.1.call-done = f32[4096,4,128]{2,0,1:T(8,128)} async-done(((f32[512,4,128]{2,0,1:T(8,128)}), f32[4096,4,128]{2,0,1:T(8,128)}) %all-gather.5.cloned.1.call-update) | async-done | bytes 8388624 | tf_op jit(solution)/shard_map/all_gather | solution.py:26
  154.7 8.1 %copy.29 = f32[16,8,32,4,128]{4,2,1,0,3:T(8,128)} copy(f32[16,8,32,4,128]{4,2,0,1,3:T(8,128)} %bitcast.156) | data formatting | bytes 16777216 | tf_op jit(solution)/shard_map/transpose | solution.py:29
  162.7 112.5 %all-gather.3.cloned.1.call-done = f32[4096,4,256]{0,2,1:T(8,128)} async-done(((f32[256,4,256]{0,2,1:T(8,128)}), f32[4096,4,256]{0,2,1:T(8,128)}) %all-gather.3.cloned.1.call-update) | async-done | bytes 16777232 | tf_op jit(solution)/shard_map/all_gather | solution.py:33
  275.3 29.7 %fusion = f32[4,256,4,128]{3,1,2,0:T(8,128)S(1)} fusion(f32[4096,4,128,1]{2,0,1,3:T(8,128)} %bitcast.157, f32[4096,4,256]{0,2,1:T(8,128)} %all-gather.3.cloned.1.call-done), kind=kOutput, calls=%fused_computation | convolution fusion | flops 25769803776 | bytes 27262976 | tf_op jit(solution)/shard_map/qia,qjb->iajb/dot_general | solution.py:10
  305.0 0.1 fusion.25
  305.1 0.1 fusion.24
  305.2 0.1 fusion.23
  305.3 0.1 fusion.22
  305.4 0.1 fusion.21
  305.5 1.0 fusion.4
  306.5 3.9 %stack.37 = f32[6]{0:T(128)S(1)} concatenate(f32[1]{0:T(128)} %bitcast.28, f32[1]{0:T(128)} %bitcast.31, f32[1]{0:T(128)} %bitcast.34, f32[1]{0:T(128)} %bitcast.37, f32[1]{0:T(128)} %bitcast.40, f32[1]{0:T(128)} %bitcast.43), dimensions={0} | concatenate | bytes 48 | tf_op jit(solution)/shard_map/stack | solution.py:46
  310.4 0.1 fusion.20
  310.5 64.2 %psum.7 = f32[6]{0:T(128)S(1)} all-reduce(f32[6]{0:T(128)S(1)} %stack.37), channel_id=1, replica_groups=mesh['row'=8,'col'=16] {'row','col'}, use_global_device_ids=true, to_apply=%region_6.0 | all-reduce | flops 6 | bytes 48 | tf_op jit(solution)/shard_map/psum | solution.py:46
  374.7 0.5 broadcast_multiply_fusion
  (7 shorter events, 0.0 us)
Async XLA Ops:
  7.2 147.5 %all-gather.5.cloned.1.call-start = ((), (), s32[]{:S(2)}) async-start(), calls=%async_computation.3 | async-start | bytes 9437184 | tf_op jit(solution)/shard_map/all_gather | solution.py:26
  54.0 221.3 %all-gather.3.cloned.1.call-start = ((), (), s32[]{:S(2)}) async-start(), calls=%async_computation.2 | async-start | bytes 17825792 | tf_op jit(solution)/shard_map/all_gather | solution.py:33
  98.1 4.9 %copy-start.1 = (f32[4]{0:T(128)S(1)}, f32[4]{0:T(128)}, u32[]{:S(2)}) copy-start(f32[4]{0:T(128)} %param.4) | copy-start | bytes 52
  310.5 64.7 %copy-start = (f32[6,256,128]{2,1,0:T(8,128)}, f32[6,256,128]{2,1,0:T(8,128)S(1)}, u32[]{:S(2)}) copy-start(f32[6,256,128]{2,1,0:T(8,128)S(1)} %fusion.20) | copy-start | bytes 2359300
Sparse Core Ops, SparseCore 0:
  54.1 100.5 all-gather.4
  157.0 118.2 all-gather.2
where the time goes:
time: 383 us; the launch traced here: 382 us
  waiting for transfers between devices  154 us (40%)
  blocking collectives  122 us (32%)
  local copies, waits for them, and re-layouts  44.4 us (12%)
  matrix products  29.7 us (8%)
  between operations  22 us (6%)
  other arithmetic  9.16 us (2%)
    all_gather x1, waiting for transfers between devices, local(): left_ops = lax.all_gather(left_part, 'col', axis=0, tiled=True)  113 us
    psum x1, blocking collectives, local(): total = lax.psum(jnp.stack(shares), ('row', 'col'))  64.2 us
    all_gather x1, waiting for transfers between devices, local(): stacked = lax.all_gather(moved, 'row', axis=0, tiled=True)  41.6 us
    all_to_all x1, blocking collectives, local(): lax.all_to_all(slab, 'row', split_axis=2, concat_axis=0, tiled=True)  32.3 us
    dot_general x1, matrix products, contract(): jnp.einsum('qia,qjb->iajb', left, right, precision=lax.Precision.HIGHEST,...  29.7 us
    all_to_all x1, blocking collectives, local(): moved = lax.all_to_all(slab, 'col', split_axis=2, concat_axis=0, tiled=True)  26 us
    unnamed x9, local copies, waits for them, and re-layouts  21.1 us
    transpose x1, local copies, waits for them, and re-layouts, local(): right_ops = stacked.reshape(n_row, n_col, per_dev, occ, wide_b).transpose...  8.06 us
  transfers between devices with their start and end apart: 2, of which 2 were waited for; matrix products, arithmetic and copies ran while one was open for 7% of the time, Pallas kernels for 0%

commit v1 on v0

v1 whole, which is shorter than its diff:
```python
import jax
import jax.numpy as jnp
from jax import lax
from jax.experimental import pallas as pl
from jax.experimental.pallas import tpu as pltpu
from jax.sharding import PartitionSpec as P

F32, BF16 = jnp.float32, jnp.bfloat16
NQ = 32
NV = 2048
SEQ = [(0, 0, 2), (0, 1, 1), (1, 0, 4), (1, 1, 3), (0, 2, 0), (2, 0, 5)]
PAIRS = [(0, 1), (0, 2), (0, 3), (1, 2), (1, 3), (2, 3)]


def kernel(
    slab, occ, vir, amps, energy,
    send_l, send_r, left, right, lt_hi, lt_lo, r_hi, r_lo,
    part, part_in, x_in, dfin, t_in, vir_a, e_acc, e_col, e_row,
    a_s, a_r, g_s, g_r, f_s, f_r, d_s, d_r, x_s, x_r, t_s, t_r, e1_s, e1_r, e2_s, e2_r,
):
    row = lax.axis_index("row")
    col = lax.axis_index("col")
    x_lo, y = row // 4, row % 4
    z, x_hi, core = col // 4, (col // 2) % 2, col % 2
    colchip = col // 2

    def at_y(d):
        return {"row": x_lo * 4 + (y + d) % 4}

    def at_z(d):
        return {"col": ((z + d) % 4) * 4 + x_hi * 2 + core}

    def at_x(d):
        xx = (x_hi * 2 + x_lo + d) % 4
        return {"row": (xx % 2) * 4 + y, "col": (z * 2 + xx // 2) * 2 + core}

    sibling = {"col": colchip * 2 + 1 - core}

    def partner(h):
        return {"row": colchip, "col": row * 2 + h}

    bar = pltpu.get_barrier_semaphore()
    for d in range(1, 8):
        pl.semaphore_signal(bar, inc=1, device_id={"row": (row + d) % 8})
    for d in range(1, 16):
        pl.semaphore_signal(bar, inc=1, device_id={"col": (col + d) % 16})
    pl.semaphore_signal(
        bar, inc=1, device_id={"row": (1 - x_lo) * 4 + y, "col": (z * 2 + 1 - x_hi) * 2 + core}
    )

    @pl.when(row != colchip)
    def _():
        for h in range(2):
            pl.semaphore_signal(bar, inc=1, device_id=partner(h))

    def stage(o):
        v = slab[:, o, :]
        for k in range(4):
            send_l[o, k, :, 0:256] = v[:, k * 256 : k * 256 + 256]
            send_l[o, k, :, 256:512] = v[:, 1024 + k * 256 : 1280 + k * 256]
        w = slab[:, 3 - o, :]
        for k in range(4):
            for c in range(2):
                for h in range(2):
                    b = k * 512 + h * 256 + c * 128
                    send_r[o, k, :, c * 256 + h * 128 : c * 256 + h * 128 + 128] = w[:, b : b + 128]
        left[o, z, y] = send_l[o, y]
        right[o, y, z] = send_r[o, z]

    stage(0)
    pl.semaphore_wait(bar, jnp.where(row == colchip, 23, 25))

    started = []

    def copy(src, dst, ssem, rsem, to):
        cp = pltpu.make_async_remote_copy(src, dst, ssem, rsem, device_id=to)
        cp.start()
        started.append(cp)
        return cp

    scatter, gather, onward = {}, {}, {}

    def post_scatter(o):
        for d in (1, 3, 2):
            ky, kz = (y + d) % 4, (z + d) % 4
            scatter[o, 0, d] = copy(
                send_l.at[o, ky], left.at[o, z, y], a_s.at[0, o, d - 1], a_r.at[0, o, d - 1], at_y(d)
            )
            scatter[o, 1, d] = copy(
                send_r.at[o, kz], right.at[o, y, z], a_s.at[1, o, d - 1], a_r.at[1, o, d - 1], at_z(d)
            )

    def post_gather(o, d):
        ky, kz = (y - d) % 4, (z - d) % 4
        for way, step in ((0, 1), (1, 3)):
            gather[o, 0, way, d] = copy(
                left.at[o, z, ky], left.at[o, z, ky], g_s.at[0, o, way, d], g_r.at[0, o, way, d], at_z(step)
            )
            gather[o, 1, way, d] = copy(
                right.at[o, y, kz], right.at[o, y, kz], g_s.at[1, o, way, d], g_r.at[1, o, way, d], at_y(step)
            )

    def rest_gather(o):
        for d in (1, 3, 2):
            scatter[o, 0, d].wait_recv()
            scatter[o, 1, d].wait_recv()
            post_gather(o, d)

    def forward(o):
        for way, step, half in ((0, 1, 0), (1, 3, 2)):
            for side in range(2):
                for d in range(4):
                    gather[o, side, way, d].wait_recv()
            kz, ky = (z - step) % 4, (y - step) % 4
            onward[o, 0, way] = copy(
                left.at[o, kz, pl.ds(half, 2)], left.at[o, kz, pl.ds(half, 2)],
                f_s.at[0, o, way], f_r.at[0, o, way], at_z(step),
            )
            onward[o, 1, way] = copy(
                right.at[o, ky, pl.ds(half, 2)], right.at[o, ky, pl.ds(half, 2)],
                f_s.at[1, o, way], f_r.at[1, o, way], at_y(step),
            )

    def prepare(o):
        for way in range(2):
            onward[o, 0, way].wait_recv()
            onward[o, 1, way].wait_recv()
        for k in range(4):
            v = left[o, k].reshape(128, 512).T
            hi = v.astype(BF16)
            lt_hi[o, :, k * 128 : k * 128 + 128] = hi
            lt_lo[o, :, k * 128 : k * 128 + 128] = (v - hi.astype(F32)).astype(BF16)
        for kz in range(4):
            for ky in range(4):
                w = right[o, ky, kz]
                hi = w.astype(BF16)
                lo = (w - hi.astype(F32)).astype(BF16)
                q = kz * 128 + ky * 32
                for h in range(2):
                    r_hi[o, h, q : q + 32, :] = hi[:, h * 256 : h * 256 + 256]
                    r_lo[o, h, q : q + 32, :] = lo[:, h * 256 : h * 256 + 256]

    def multiply(s, which, half):
        lo_, ro_, _ = SEQ[s]

        @pl.loop(0, 2)
        def _(ab):
            rows = pl.ds(pl.multiple_of(ab * 256, 256), 256)
            hi = lt_hi[lo_, rows, :]
            acc = jnp.dot(hi, r_hi[ro_, half], preferred_element_type=F32)
            acc += jnp.dot(hi, r_lo[ro_, half], preferred_element_type=F32)
            acc += jnp.dot(lt_lo[lo_, rows, :], r_hi[ro_, half], preferred_element_type=F32)
            part[s, which, ab] = acc[:, 0:128]
            part[s, which, 2 + ab] = acc[:, 128:256]

    exchanged, along_x = {}, {}
    me_x = x_hi * 2 + x_lo

    def compute(s):
        multiply(s, 0, 1 - core)
        exchanged[s] = copy(part.at[s, 0], part_in.at[s], d_s.at[s], d_r.at[s], sibling)
        multiply(s, 1, core)

    def reduce(s):
        exchanged[s].wait_recv()
        part[s, 1] = part[s, 1] + part_in[s]
        for d in (1, 3, 2):
            along_x[s, d] = copy(
                part.at[s, 1, (me_x + d) % 4], x_in.at[s, d - 1], x_s.at[s, d - 1], x_r.at[s, d - 1], at_x(d)
            )

    def swap(s, h):
        return pltpu.make_async_remote_copy(
            dfin.at[s, pl.ds(pl.multiple_of(h * 128, 128), 128)], t_in.at[s, core], t_s.at[s, h], t_r.at[s, core],
            device_id=partner(h),
        )

    def swap_sibling(s):
        return pltpu.make_async_remote_copy(
            dfin.at[s, pl.ds(pl.multiple_of((1 - core) * 128, 128), 128)], t_in.at[s, core],
            t_s.at[s, 0], t_r.at[s, core], device_id=sibling,
        )

    def sends(s):
        return row < colchip if s % 2 == 0 else row > colchip

    def receives(s):
        return row > colchip if s % 2 == 0 else row < colchip

    vir_b = vir[pl.ds(col, 1), :]

    def finish(s):
        for d in range(1, 4):
            along_x[s, d].wait_recv()
        p = SEQ[s][2]
        i, j = PAIRS[p]
        total = (part[s, 1, me_x] + x_in[s, 0]) + (x_in[s, 1] + x_in[s, 2])
        dfin[s] = total

        @pl.when(sends(s))
        def _():
            for h in range(2):
                swap(s, h).start()

        @pl.when(row == colchip)
        def _():
            swap_sibling(s).start()
            t_in[s, core] = dfin[s, pl.ds(pl.multiple_of(core * 128, 128), 128), :]

        amp = total / (((occ[i] + occ[j]) - vir_a[...]) - vir_b)
        amps[p] = amp
        e_acc[p] = jnp.sum((2.0 * (amp * total)).reshape(32, 8, 128), axis=0)

    def energy_swapped(s, weight):
        p = SEQ[s][2]
        prod = amps[p, 0:128] * t_in[s, 0].T + amps[p, 128:256] * t_in[s, 1].T
        e_acc[p] = e_acc[p] - weight * jnp.sum(prod.reshape(16, 8, 128), axis=0)

    def swapped(s):
        @pl.when(receives(s))
        def _():
            for h in range(2):
                pltpu.make_async_remote_copy(
                    t_in.at[s, h], t_in.at[s, h], t_s.at[s, h], t_r.at[s, h], device_id=sibling
                ).wait_recv()
            energy_swapped(s, 2.0)

        @pl.when(row == colchip)
        def _():
            pltpu.make_async_remote_copy(
                t_in.at[s, 1 - core], t_in.at[s, 1 - core], t_s.at[s, 0], t_r.at[s, 1 - core], device_id=sibling
            ).wait_recv()
            energy_swapped(s, 1.0)
            swap_sibling(s).wait_send()

        @pl.when(sends(s))
        def _():
            for h in range(2):
                swap(s, h).wait_send()

    post_scatter(0)
    post_gather(0, 0)
    stage(1)
    rest_gather(0)
    post_scatter(1)
    post_gather(1, 0)
    stage(2)
    for h in range(2):
        vir_a[h * 128 : h * 128 + 128, :] = jnp.broadcast_to(vir[pl.ds(row * 2 + h, 1), :], (128, 128)).T
    forward(0)
    rest_gather(1)
    post_scatter(2)
    post_gather(2, 0)
    prepare(0)
    compute(0)
    forward(1)
    rest_gather(2)
    reduce(0)
    prepare(1)
    compute(1)
    compute(2)
    reduce(1)
    compute(3)
    reduce(2)
    reduce(3)
    forward(2)
    finish(0)
    swapped(0)
    prepare(2)
    compute(4)
    compute(5)
    reduce(4)
    reduce(5)
    for s in range(1, 6):
        finish(s)
    for s in range(1, 6):
        swapped(s)

    e_tile = jnp.concatenate(
        [jnp.sum(e_acc[p], axis=0, keepdims=True) for p in range(6)] + [jnp.zeros((2, 128), F32)], axis=0
    )
    e_col[col] = e_tile
    hops = []
    for d in range(1, 16):
        hops.append(copy(e_col.at[col], e_col.at[col], e1_s.at[d - 1], e1_r.at[d - 1], {"col": (col + d) % 16}))
    for cp in hops:
        cp.wait_recv()
    e_row[row] = jnp.sum(e_col[...], axis=0)
    hops = []
    for d in range(1, 8):
        hops.append(copy(e_row.at[row], e_row.at[row], e2_s.at[d - 1], e2_r.at[d - 1], {"row": (row + d) % 8}))
    for cp in hops:
        cp.wait_recv()
    whole = jnp.sum(jnp.sum(e_row[...], axis=0), axis=1, keepdims=True)
    energy[...] = jnp.broadcast_to(whole * (2.0 / (NV * NV)), (8, 128))
    for cp in started:
        cp.wait_send()


def local(slab, occ_energy, vir_energy):
    dma = pltpu.SemaphoreType.DMA
    vmem = pltpu.VMEM
    both = lambda *shape: [dma(shape), dma(shape)]
    amps, energy = pl.pallas_call(
        kernel,
        out_shape=(
            jax.ShapeDtypeStruct((6, 256, 128), F32),
            jax.ShapeDtypeStruct((8, 128), F32),
        ),
        in_specs=[
            pl.BlockSpec(memory_space=vmem),
            pl.BlockSpec(memory_space=pltpu.SMEM),
            pl.BlockSpec(memory_space=vmem),
        ],
        out_specs=(pl.BlockSpec(memory_space=vmem), pl.BlockSpec(memory_space=vmem)),
        scratch_shapes=[
            vmem((3, 4, NQ, 512), F32),
            vmem((3, 4, NQ, 512), F32),
            vmem((3, 4, 4, NQ, 512), F32),
            vmem((3, 4, 4, NQ, 512), F32),
            vmem((3, 512, 512), BF16),
            vmem((3, 512, 512), BF16),
            vmem((3, 2, 512, 256), BF16),
            vmem((3, 2, 512, 256), BF16),
            vmem((6, 2, 4, 256, 128), F32),
            vmem((6, 4, 256, 128), F32),
            vmem((6, 3, 256, 128), F32),
            vmem((6, 256, 128), F32),
            vmem((6, 2, 128, 128), F32),
            vmem((256, 128), F32),
            vmem((6, 8, 128), F32),
            vmem((16, 8, 128), F32),
            vmem((8, 8, 128), F32),
            *both(2, 3, 3),
            *both(2, 3, 2, 4),
            *both(2, 3, 2),
            *both(6),
            *both(6, 3),
            *both(6, 2),
            *both(15),
            *both(7),
        ],
        compiler_params=pltpu.CompilerParams(
            collective_id=0, has_side_effects=True, vmem_limit_bytes=48 * 2**20
        ),
        name="pairs",
    )(slab, occ_energy, vir_energy.reshape(16, 128))
    return amps, energy[:6, 0]


def solution(mesh):
    return jax.shard_map(
        local,
        mesh=mesh,
        in_specs=(P(("row", "col"), None, None), P(), P()),
        out_specs=(P(None, "row", "col"), P()),
        check_vma=False,
    )
```

time: 383 us -> 118 us (0.31)
  waiting for transfers between devices: 154 us -> 0 us
  blocking collectives: 122 us -> 0 us
  Pallas kernels: 0 us -> 113 us
  local copies, waits for them, and re-layouts: 44.4 us -> 4.07 us
  matrix products: 29.7 us -> 0 us
  between operations: 22 us -> 0.65 us
  other arithmetic: 9.16 us -> 0 us
    all_gather x2 -> x0, waiting for transfers between devices: 154 us -> none  [the longest x1 113 us: local(): left_ops = lax.all_gather(left_part, 'col', axis=0, tiled=True)]
    pallas_call x0 -> x1, Pallas kernels: none -> 113 us  [local(): pl.pallas_call(kernel, out_shape=(jax.ShapeDtypeStruct((6, 256, 128), F32...]
    psum x1 -> x0, blocking collectives: 64.2 us -> none  [local(): total = lax.psum(jnp.stack(shares), ('row', 'col'))]
    all_to_all x2 -> x0, blocking collectives: 58.3 us -> none  [the longest x1 32.3 us: local(): lax.all_to_all(slab, 'row', split_axis=2, concat_axis=0, tiled=True)]
    dot_general x1 -> x0, matrix products: 29.7 us -> none  [contract(): jnp.einsum('qia,qjb->iajb', left, right, precision=lax.Precision.HIGHEST,...]
    unnamed x9 -> x7, local copies, waits for them, and re-layouts: 21.1 us -> 3.45 us
    all_to_all x4 -> x0, local copies, waits for them, and re-layouts: 9.9 us -> none  [the longest x2 5.07 us: local(): moved = lax.all_to_all(slab, 'col', split_axis=2, concat_axis=0, tiled=True)]
    transpose x1 -> x0, local copies, waits for them, and re-layouts: 8.06 us -> none  [local(): right_ops = stacked.reshape(n_row, n_col, per_dev, occ, wide_b).transpose...]
  transfers between devices with their start and end apart: 2 -> 0, of which waited for: 2 -> 0; matrix products, arithmetic and copies ran while one was open for 7% -> 0% of each run, Pallas kernels for 0% -> 0%
where the time goes in v1:
time: 118 us
  Pallas kernels  113 us (96%)
  local copies, waits for them, and re-layouts  4.07 us (3%)
    pallas_call x1, Pallas kernels, local(): pl.pallas_call(kernel, out_shape=(jax.ShapeDtypeStruct((6, 256, 128), F32...  113 us
    unnamed x7, local copies, waits for them, and re-layouts  3.45 us

profile of v1, /device:TPU:1, one launch (start us, length us, event | category | flops | bytes accessed | tf_op | source)
XLA Modules:
  0.0 117.8 jit_solution(833698999567265082)
XLA Ops:
  0.6 0.0 copy-start.2
  0.6 0.6 copy-done.2
  1.3 0.0 copy-start
  1.3 1.2 %copy-done = f32[32,4,2048]{2,1,0:T(4,128)S(1)} copy-done((f32[32,4,2048]{2,1,0:T(4,128)S(1)}, f32[32,4,2048]{2,1,0:T(4,128)}, u32[]{:S(2)}) %copy-start) | copy-done | bytes 1048600
  2.5 0.0 copy-start.1
  2.5 0.7 copy-done.1
  3.2 113.1 %pairs.1 = (f32[6,256,128]{2,1,0:T(8,128)S(1)}, f32[8,128]{1,0:T(8,128)S(1)}) custom-call(f32[32,4,2048]{2,1,0:T(4,128)S(1)} %copy-done, f32[4]{0:T(128)S(1)} %copy-done.2, f32[16,128]{1,0:T(8,128)S(1)} %bitcast.1), custom_call_target="tpu_custom_call" | custom-call | tf_op jit(solution)/shard_map/pairs/pallas_call | solution.py:304
  116.3 0.6 slice_reduce_fusion
  117.0 0.9 copy.6
Async XLA Ops:
  0.6 0.7 copy-start.2
  1.3 1.2 %copy-start = (f32[32,4,2048]{2,1,0:T(4,128)S(1)}, f32[32,4,2048]{2,1,0:T(4,128)}, u32[]{:S(2)}) copy-start(f32[32,4,2048]{2,1,0:T(4,128)} %slab.1) | copy-start | bytes 3145732
  2.5 0.7 copy-start.1

commit v2 on v1

--- a/solution.py
+++ b/solution.py
@@ -15,7 +15,7 @@
 def kernel(
     slab, occ, vir, amps, energy,
     send_l, send_r, left, right, lt_hi, lt_lo, r_hi, r_lo,
-    part, part_in, x_in, dfin, t_in, vir_a, e_acc, e_col, e_row,
+    part, part_in, x_in, x_via, dfin, t_in, vir_a, e_acc, e_col, e_row,
     a_s, a_r, g_s, g_r, f_s, f_r, d_s, d_r, x_s, x_r, t_s, t_r, e1_s, e1_r, e2_s, e2_r,
 ):
     row = lax.axis_index("row")
@@ -106,25 +106,24 @@
             scatter[o, 1, d].wait_recv()
             post_gather(o, d)
 
-    def forward(o):
-        for way, step, half in ((0, 1, 0), (1, 3, 2)):
-            for side in range(2):
-                for d in range(4):
-                    gather[o, side, way, d].wait_recv()
-            kz, ky = (z - step) % 4, (y - step) % 4
-            onward[o, 0, way] = copy(
-                left.at[o, kz, pl.ds(half, 2)], left.at[o, kz, pl.ds(half, 2)],
-                f_s.at[0, o, way], f_r.at[0, o, way], at_z(step),
-            )
-            onward[o, 1, way] = copy(
-                right.at[o, ky, pl.ds(half, 2)], right.at[o, ky, pl.ds(half, 2)],
-                f_s.at[1, o, way], f_r.at[1, o, way], at_y(step),
-            )
+    def forward(o, d):
+        way, step = (0, 1) if d % 2 == 0 else (1, 3)
+        kz, ky = (z - step) % 4, (y - step) % 4
+        jy, jz = (y - d) % 4, (z - d) % 4
+        gather[o, 0, way, d].wait_recv()
+        onward[o, 0, d] = copy(
+            left.at[o, kz, jy], left.at[o, kz, jy], f_s.at[0, o, d], f_r.at[0, o, d], at_z(step)
+        )
+        gather[o, 1, way, d].wait_recv()
+        onward[o, 1, d] = copy(
+            right.at[o, ky, jz], right.at[o, ky, jz], f_s.at[1, o, d], f_r.at[1, o, d], at_y(step)
+        )
 
     def prepare(o):
-        for way in range(2):
-            onward[o, 0, way].wait_recv()
-            onward[o, 1, way].wait_recv()
+        for side in range(2):
+            for d in range(4):
+                gather[o, side, 1 - (d % 2), d].wait_recv()
+                onward[o, side, d].wait_recv()
         for k in range(4):
             v = left[o, k].reshape(128, 512).T
             hi = v.astype(BF16)
@@ -161,13 +160,26 @@
         exchanged[s] = copy(part.at[s, 0], part_in.at[s], d_s.at[s], d_r.at[s], sibling)
         multiply(s, 1, core)
 
+    up_x, down_x, far_x = (me_x + 1) % 4, (me_x + 3) % 4, (me_x + 2) % 4
+    low, high = pl.ds(0, 128), pl.ds(128, 128)
+
     def reduce(s):
         exchanged[s].wait_recv()
         part[s, 1] = part[s, 1] + part_in[s]
-        for d in (1, 3, 2):
-            along_x[s, d] = copy(
-                part.at[s, 1, (me_x + d) % 4], x_in.at[s, d - 1], x_s.at[s, d - 1], x_r.at[s, d - 1], at_x(d)
-            )
+        mine = part.at[s, 1]
+        along_x[s, 0] = copy(mine.at[far_x, low], x_via.at[s, 0], x_s.at[s, 0], x_r.at[s, 0], at_x(1))
+        along_x[s, 1] = copy(mine.at[far_x, high], x_via.at[s, 1], x_s.at[s, 1], x_r.at[s, 1], at_x(3))
+        along_x[s, 2] = copy(mine.at[up_x, high], x_in.at[s, 0, high], x_s.at[s, 2], x_r.at[s, 2], at_x(1))
+        along_x[s, 3] = copy(mine.at[down_x, low], x_in.at[s, 1, low], x_s.at[s, 3], x_r.at[s, 3], at_x(3))
+
+    def reduce_on(s):
+        mine = part.at[s, 1]
+        along_x[s, 0].wait_recv()
+        part[s, 1, up_x, 0:128] = part[s, 1, up_x, 0:128] + x_via[s, 0]
+        along_x[s, 4] = copy(mine.at[up_x, low], x_in.at[s, 0, low], x_s.at[s, 4], x_r.at[s, 4], at_x(1))
+        along_x[s, 1].wait_recv()
+        part[s, 1, down_x, 128:256] = part[s, 1, down_x, 128:256] + x_via[s, 1]
+        along_x[s, 5] = copy(mine.at[down_x, high], x_in.at[s, 1, high], x_s.at[s, 5], x_r.at[s, 5], at_x(3))
 
     def swap(s, h):
         return pltpu.make_async_remote_copy(
@@ -190,11 +202,11 @@
     vir_b = vir[pl.ds(col, 1), :]
 
     def finish(s):
-        for d in range(1, 4):
-            along_x[s, d].wait_recv()
+        for k in range(2, 6):
+            along_x[s, k].wait_recv()
         p = SEQ[s][2]
         i, j = PAIRS[p]
-        total = (part[s, 1, me_x] + x_in[s, 0]) + (x_in[s, 1] + x_in[s, 2])
+        total = part[s, 1, me_x] + (x_in[s, 0] + x_in[s, 1])
         dfin[s] = total
 
         @pl.when(sends(s))
@@ -238,43 +250,61 @@
             for h in range(2):
                 swap(s, h).wait_send()
 
+    def forward_rest(o):
+        for d in (1, 3, 2):
+            forward(o, d)
+
     post_scatter(0)
     post_gather(0, 0)
     stage(1)
     rest_gather(0)
+    forward(0, 0)
     post_scatter(1)
     post_gather(1, 0)
     stage(2)
     for h in range(2):
         vir_a[h * 128 : h * 128 + 128, :] = jnp.broadcast_to(vir[pl.ds(row * 2 + h, 1), :], (128, 128)).T
-    forward(0)
+    forward_rest(0)
     rest_gather(1)
+    forward(1, 0)
     post_scatter(2)
     post_gather(2, 0)
     prepare(0)
     compute(0)
-    forward(1)
+    reduce(0)
+    forward_rest(1)
+    reduce_on(0)
     rest_gather(2)
-    reduce(0)
+    forward(2, 0)
     prepare(1)
     compute(1)
     compute(2)
     reduce(1)
+    finish(0)
     compute(3)
     reduce(2)
+    reduce_on(1)
     reduce(3)
-    forward(2)
-    finish(0)
-    swapped(0)
+    reduce_on(2)
+    forward_rest(2)
+    reduce_on(3)
+    finish(1)
+    finish(2)
+    finish(3)
     prepare(2)
     compute(4)
     compute(5)
     reduce(4)
     reduce(5)
-    for s in range(1, 6):
-        finish(s)
-    for s in range(1, 6):
+    swapped(0)
+    reduce_on(4)
+    reduce_on(5)
+    for s in range(1, 4):
         swapped(s)
+    finish(4)
+    finish(5)
+    swapped(4)
+    swapped(5)
 
     e_tile = jnp.concatenate(
         [jnp.sum(e_acc[p], axis=0, keepdims=True) for p in range(6)] + [jnp.zeros((2, 128), F32)], axis=0
@@ -324,7 +354,8 @@
             vmem((3, 2, 512, 256), BF16),
             vmem((6, 2, 4, 256, 128), F32),
             vmem((6, 4, 256, 128), F32),
-            vmem((6, 3, 256, 128), F32),
+            vmem((6, 2, 256, 128), F32),
+            vmem((6, 2, 128, 128), F32),
             vmem((6, 256, 128), F32),
             vmem((6, 2, 128, 128), F32),
             vmem((256, 128), F32),
@@ -333,9 +364,9 @@
             vmem((8, 8, 128), F32),
             *both(2, 3, 3),
             *both(2, 3, 2, 4),
-            *both(2, 3, 2),
+            *both(2, 3, 4),
             *both(6),
-            *both(6, 3),
+            *both(6, 6),
             *both(6, 2),
             *both(15),
             *both(7),

time: 118 us -> 104 us (0.88)
  Pallas kernels: 113 us -> 99.1 us
    pallas_call x1, Pallas kernels: 113 us -> 99.1 us  [local(): pl.pallas_call(kernel, out_shape=(jax.ShapeDtypeStruct((6, 256, 128), F32...]
where the time goes in v2:
time: 104 us
  Pallas kernels  99.1 us (95%)
  local copies, waits for them, and re-layouts  4.07 us (4%)
    pallas_call x1, Pallas kernels, local(): pl.pallas_call(kernel, out_shape=(jax.ShapeDtypeStruct((6, 256, 128), F32...  99.1 us
    unnamed x7, local copies, waits for them, and re-layouts  3.45 us

profile of v2, /device:TPU:1, one launch (start us, length us, event | category | flops | bytes accessed | tf_op | source)
XLA Modules:
  0.0 103.9 jit_solution(3979560040921095400)
XLA Ops:
  0.6 0.0 copy-start.2
  0.6 0.6 copy-done.2
  1.3 0.0 copy-start
  1.3 1.2 %copy-done = f32[32,4,2048]{2,1,0:T(4,128)S(1)} copy-done((f32[32,4,2048]{2,1,0:T(4,128)S(1)}, f32[32,4,2048]{2,1,0:T(4,128)}, u32[]{:S(2)}) %copy-start) | copy-done | bytes 1048600
  2.5 0.0 copy-start.1
  2.5 0.7 copy-done.1
  3.2 99.1 %pairs.1 = (f32[6,256,128]{2,1,0:T(8,128)S(1)}, f32[8,128]{1,0:T(8,128)S(1)}) custom-call(f32[32,4,2048]{2,1,0:T(4,128)S(1)} %copy-done, f32[4]{0:T(128)S(1)} %copy-done.2, f32[16,128]{1,0:T(8,128)S(1)} %bitcast.1), custom_call_target="tpu_custom_call" | custom-call | tf_op jit(solution)/shard_map/pairs/pallas_call | solution.py:334
  102.4 0.6 slice_reduce_fusion
  103.0 0.9 copy.6
Async XLA Ops:
  0.6 0.7 copy-start.2
  1.3 1.2 %copy-start = (f32[32,4,2048]{2,1,0:T(4,128)S(1)}, f32[32,4,2048]{2,1,0:T(4,128)}, u32[]{:S(2)}) copy-start(f32[32,4,2048]{2,1,0:T(4,128)} %slab.1) | copy-start | bytes 3145732
  2.5 0.7 copy-start.1

commit v3 on v2

--- a/solution.py
+++ b/solution.py
@@ -15,8 +15,8 @@
 def kernel(
     slab, occ, vir, amps, energy,
     send_l, send_r, left, right, lt_hi, lt_lo, r_hi, r_lo,
-    part, part_in, x_in, x_via, dfin, t_in, vir_a, e_acc, e_col, e_row,
-    a_s, a_r, g_s, g_r, f_s, f_r, d_s, d_r, x_s, x_r, t_s, t_r, e1_s, e1_r, e2_s, e2_r,
+    part, part_in, x_in, x_via, dfin, t_in, via, vir_a, e_acc, e_col, e_row,
+    a_s, a_r, g_s, g_r, f_s, f_r, d_s, d_r, x_s, x_r, t_s, t_r, v_s, v_r, e1_s, e1_r, e2_s, e2_r,
 ):
     row = lax.axis_index("row")
     col = lax.axis_index("col")
@@ -52,6 +52,28 @@
     def _():
         for h in range(2):
             pl.semaphore_signal(bar, inc=1, device_id=partner(h))
+
+    me_x = x_hi * 2 + x_lo
+    relay_row = x_lo * 4 + colchip % 4
+    relay_chip = (row // 2) * 2 + x_hi
+    to_x = (row % 2) * 2 + colchip // 4
+    hop_x = (to_x - me_x + 4) % 4
+    by_relay = (hop_x != 0) & ((relay_row != row) | (relay_chip != colchip))
+
+    def source(k):
+        xx = (me_x + k) % 4
+        y_s = (z % 2) * 2 + xx // 2
+        z_s = (xx % 2) * 2 + y // 2
+        there = (x_hi == y % 2) & (x_lo == z // 2) & ((y_s != y) | (z_s != z))
+        return x_lo * 4 + y_s, z_s * 2 + x_hi, there
+
+    for k in range(1, 4):
+        row_s, chip_s, there = source(k)
+
+        @pl.when(there)
+        def _():
+            for h in range(2):
+                pl.semaphore_signal(bar, inc=1, device_id={"row": row_s, "col": chip_s * 2 + h})
 
     def stage(o):
         v = slab[:, o, :]
@@ -68,7 +90,7 @@
         right[o, y, z] = send_r[o, z]
 
     stage(0)
-    pl.semaphore_wait(bar, jnp.where(row == colchip, 23, 25))
+    pl.semaphore_wait(bar, 23 + jnp.where(row == colchip, 0, 2) + jnp.where(by_relay, 2, 0))
 
     started = []
 
@@ -153,7 +175,6 @@
             part[s, which, 2 + ab] = acc[:, 128:256]
 
     exchanged, along_x = {}, {}
-    me_x = x_hi * 2 + x_lo
 
     def compute(s):
         multiply(s, 0, 1 - core)
@@ -181,16 +202,46 @@
         part[s, 1, down_x, 128:256] = part[s, 1, down_x, 128:256] + x_via[s, 1]
         along_x[s, 5] = copy(mine.at[down_x, high], x_in.at[s, 1, high], x_s.at[s, 5], x_r.at[s, 5], at_x(3))
 
-    def swap(s, h):
+    def swap(s, h, part_no):
+        rows = pl.ds(pl.multiple_of(h * 128 + part_no * 64, 64), 64)
         return pltpu.make_async_remote_copy(
-            dfin.at[s, pl.ds(pl.multiple_of(h * 128, 128), 128)], t_in.at[s, core], t_s.at[s, h], t_r.at[s, core],
-            device_id=partner(h),
-        )
+            dfin.at[s, rows], t_in.at[s, core, pl.ds(part_no * 64, 64)],
+            t_s.at[s, h, part_no], t_r.at[s, core, part_no], device_id=partner(h),
+        )
+
+    def swap_by_relay(s, h):
+        rows = pl.ds(pl.multiple_of(h * 128 + 64, 64), 64)
+        return pltpu.make_async_remote_copy(
+            dfin.at[s, rows], via.at[s, hop_x - 1, core], t_s.at[s, h, 1], v_r.at[s, hop_x - 1, core],
+            device_id={"row": relay_row, "col": relay_chip * 2 + h},
+        )
+
+    def onto(s, k, c):
+        row_s, chip_s, _ = source(k)
+        return pltpu.make_async_remote_copy(
+            via.at[s, k - 1, c], t_in.at[s, c, pl.ds(64, 64)], v_s.at[s, k - 1, c], t_r.at[s, c, 1],
+            device_id={"row": chip_s, "col": row_s * 2 + core},
+        )
+
+    def relays(s, k):
+        row_s, chip_s, there = source(k)
+        return there & (row_s < chip_s if s % 2 == 0 else row_s > chip_s)
+
+    def relay(s):
+        for k in range(1, 4):
+
+            @pl.when(relays(s, k))
+            def _():
+                for c in range(2):
+                    pltpu.make_async_remote_copy(
+                        via.at[s, k - 1, c], via.at[s, k - 1, c], v_s.at[s, k - 1, c], v_r.at[s, k - 1, c], device_id=sibling
+                    ).wait_recv()
+                    onto(s, k, c).start()
 
     def swap_sibling(s):
         return pltpu.make_async_remote_copy(
             dfin.at[s, pl.ds(pl.multiple_of((1 - core) * 128, 128), 128)], t_in.at[s, core],
-            t_s.at[s, 0], t_r.at[s, core], device_id=sibling,
+            t_s.at[s, 0, 0], t_r.at[s, core, 0], device_id=sibling,
         )
 
     def sends(s):
@@ -209,19 +260,48 @@
         total = part[s, 1, me_x] + (x_in[s, 0] + x_in[s, 1])
         dfin[s] = total
 
-        @pl.when(sends(s))
-        def _():
-            for h in range(2):
-                swap(s, h).start()
-
-        @pl.when(row == colchip)
-        def _():
-            swap_sibling(s).start()
-            t_in[s, core] = dfin[s, pl.ds(pl.multiple_of(core * 128, 128), 128), :]
-
         amp = total / (((occ[i] + occ[j]) - vir_a[...]) - vir_b)
         amps[p] = amp
         e_acc[p] = jnp.sum((2.0 * (amp * total)).reshape(32, 8, 128), axis=0)
+
+    def swap_start(s):
+        @pl.when(sends(s))
+        def _():
+            for h in range(2):
+                swap(s, h, 0).start()
+
+        @pl.when(sends(s) & by_relay)
+        def _():
+            for h in range(2):
+                swap_by_relay(s, h).start()
+
+        @pl.when(sends(s) & jnp.logical_not(by_relay))
+        def _():
+            for h in range(2):
+                swap(s, h, 1).start()
+
+        @pl.when(row == colchip)
+        def _():
+            swap_sibling(s).start()
+            t_in[s, core] = dfin[s, pl.ds(pl.multiple_of(core * 128, 128), 128), :]
+
+    def swap_sent(s):
+        @pl.when(sends(s))
+        def _():
+            for h in range(2):
+                for n in range(2):
+                    swap(s, h, n).wait_send()
+
+        @pl.when(row == colchip)
+        def _():
+            swap_sibling(s).wait_send()
+
+        for k in range(1, 4):
+
+            @pl.when(relays(s, k))
+            def _():
+                for c in range(2):
+                    onto(s, k, c).wait_send()
 
     def energy_swapped(s, weight):
         p = SEQ[s][2]
@@ -232,23 +312,19 @@
         @pl.when(receives(s))
         def _():
             for h in range(2):
-                pltpu.make_async_remote_copy(
-                    t_in.at[s, h], t_in.at[s, h], t_s.at[s, h], t_r.at[s, h], device_id=sibling
-                ).wait_recv()
+                for n in range(2):
+                    half = t_in.at[s, h, pl.ds(n * 64, 64)]
+                    pltpu.make_async_remote_copy(
+                        half, half, t_s.at[s, h, n], t_r.at[s, h, n], device_id=sibling
+                    ).wait_recv()
             energy_swapped(s, 2.0)
 
         @pl.when(row == colchip)
         def _():
             pltpu.make_async_remote_copy(
-                t_in.at[s, 1 - core], t_in.at[s, 1 - core], t_s.at[s, 0], t_r.at[s, 1 - core], device_id=sibling
+                t_in.at[s, 1 - core], t_in.at[s, 1 - core], t_s.at[s, 0, 0], t_r.at[s, 1 - core, 0], device_id=sibling
             ).wait_recv()
             energy_swapped(s, 1.0)
-            swap_sibling(s).wait_send()
-
-        @pl.when(sends(s))
-        def _():
-            for h in range(2):
-                swap(s, h).wait_send()
 
     def forward_rest(o):
         for d in (1, 3, 2):
@@ -276,33 +352,41 @@
     reduce_on(0)
     rest_gather(2)
     forward(2, 0)
+    finish(0)
     prepare(1)
     compute(1)
     compute(2)
     reduce(1)
-    finish(0)
     compute(3)
     reduce(2)
+    reduce(3)
+    forward_rest(2)
+    swap_start(0)
     reduce_on(1)
-    reduce(3)
     reduce_on(2)
-    forward_rest(2)
     reduce_on(3)
-    finish(1)
-    finish(2)
-    finish(3)
     prepare(2)
     compute(4)
     compute(5)
     reduce(4)
     reduce(5)
+    for s in range(1, 4):
+        finish(s)
+        swap_start(s)
+        relay(s - 1)
+    reduce_on(4)
     swapped(0)
-    reduce_on(4)
     reduce_on(5)
-    for s in range(1, 4):
-        swapped(s)
+    swapped(1)
+    relay(3)
+    swapped(2)
     finish(4)
+    swap_start(4)
     finish(5)
+    swap_start(5)
+    swapped(3)
+    relay(4)
+    relay(5)
     swapped(4)
     swapped(5)
 
@@ -313,6 +397,11 @@
     hops = []
     for d in range(1, 16):
         hops.append(copy(e_col.at[col], e_col.at[col], e1_s.at[d - 1], e1_r.at[d - 1], {"col": (col + d) % 16}))
+    for cp in started[: -len(hops)]:
+        cp.wait_send()
+    del started[: -len(hops)]
+    for s in range(6):
+        swap_sent(s)
     for cp in hops:
         cp.wait_recv()
     e_row[row] = jnp.sum(e_col[...], axis=0)
@@ -358,6 +447,7 @@
             vmem((6, 2, 128, 128), F32),
             vmem((6, 256, 128), F32),
             vmem((6, 2, 128, 128), F32),
+            vmem((6, 3, 2, 64, 128), F32),
             vmem((256, 128), F32),
             vmem((6, 8, 128), F32),
             vmem((16, 8, 128), F32),
@@ -367,7 +457,8 @@
             *both(2, 3, 4),
             *both(6),
             *both(6, 6),
-            *both(6, 2),
+            *both(6, 2, 2),
+            *both(6, 3, 2),
             *both(15),
             *both(7),
         ],

time: 104 us -> 100 us (0.962)
  Pallas kernels: 99.1 us -> 95.4 us
    pallas_call x1, Pallas kernels: 99.1 us -> 95.4 us  [local(): pl.pallas_call(kernel, out_shape=(jax.ShapeDtypeStruct((6, 256, 128), F32...]
where the time goes in v3:
time: 100 us
  Pallas kernels  95.4 us (95%)
  local copies, waits for them, and re-layouts  4.07 us (4%)
    pallas_call x1, Pallas kernels, local(): pl.pallas_call(kernel, out_shape=(jax.ShapeDtypeStruct((6, 256, 128), F32...  95.4 us
    unnamed x7, local copies, waits for them, and re-layouts  3.45 us

profile of v3, /device:TPU:1, one launch (start us, length us, event | category | flops | bytes accessed | tf_op | source)
XLA Modules:
  0.0 100.1 jit_solution(9296288917174926619)
XLA Ops:
  0.6 0.0 copy-start.2
  0.6 0.6 copy-done.2
  1.3 0.0 copy-start
  1.3 1.2 %copy-done = f32[32,4,2048]{2,1,0:T(4,128)S(1)} copy-done((f32[32,4,2048]{2,1,0:T(4,128)S(1)}, f32[32,4,2048]{2,1,0:T(4,128)}, u32[]{:S(2)}) %copy-start) | copy-done | bytes 1048600
  2.5 0.0 copy-start.1
  2.5 0.7 copy-done.1
  3.2 95.4 %pairs.1 = (f32[6,256,128]{2,1,0:T(8,128)S(1)}, f32[8,128]{1,0:T(8,128)S(1)}) custom-call(f32[32,4,2048]{2,1,0:T(4,128)S(1)} %copy-done, f32[4]{0:T(128)S(1)} %copy-done.2, f32[16,128]{1,0:T(8,128)S(1)} %bitcast.1), custom_call_target="tpu_custom_call" | custom-call | tf_op jit(solution)/shard_map/pairs/pallas_call | solution.py:423
  98.6 0.6 slice_reduce_fusion
  99.3 0.9 copy.6
Async XLA Ops:
  0.6 0.7 copy-start.2
  1.3 1.2 %copy-start = (f32[32,4,2048]{2,1,0:T(4,128)S(1)}, f32[32,4,2048]{2,1,0:T(4,128)}, u32[]{:S(2)}) copy-start(f32[32,4,2048]{2,1,0:T(4,128)} %slab.1) | copy-start | bytes 3145732
  2.5 0.7 copy-start.1

commit v4 on v3

--- a/solution.py
+++ b/solution.py
@@ -13,10 +13,11 @@
 
 
 def kernel(
-    slab, occ, vir, amps, energy,
+    slab_hbm, occ_hbm, vir_hbm, amps_hbm, energy,
+    slab, occ, vir, amps,
     send_l, send_r, left, right, lt_hi, lt_lo, r_hi, r_lo,
     part, part_in, x_in, x_via, dfin, t_in, via, vir_a, e_acc, e_col, e_row,
-    a_s, a_r, g_s, g_r, f_s, f_r, d_s, d_r, x_s, x_r, t_s, t_r, v_s, v_r, e1_s, e1_r, e2_s, e2_r,
+    a_s, a_r, g_s, g_r, u_r, f_s, d_s, d_r, x_s, x_r, t_s, t_r, v_s, v_r, e1_s, e1_r, e2_s, e2_r, i_s, o_s,
 ):
     row = lax.axis_index("row")
     col = lax.axis_index("col")
@@ -39,6 +40,12 @@
     def partner(h):
         return {"row": colchip, "col": row * 2 + h}
 
+    inputs = [
+        pltpu.make_async_copy(src, dst, i_s.at[n])
+        for n, (src, dst) in enumerate([(slab_hbm, slab), (occ_hbm, occ), (vir_hbm, vir)])
+    ]
+    for cp in inputs:
+        cp.start()
     bar = pltpu.get_barrier_semaphore()
     for d in range(1, 8):
         pl.semaphore_signal(bar, inc=1, device_id={"row": (row + d) % 8})
@@ -89,38 +96,37 @@
         left[o, z, y] = send_l[o, y]
         right[o, y, z] = send_r[o, z]
 
+    for cp in inputs:
+        cp.wait()
     stage(0)
     pl.semaphore_wait(bar, 23 + jnp.where(row == colchip, 0, 2) + jnp.where(by_relay, 2, 0))
-
-    started = []
 
     def copy(src, dst, ssem, rsem, to):
         cp = pltpu.make_async_remote_copy(src, dst, ssem, rsem, device_id=to)
         cp.start()
-        started.append(cp)
         return cp
 
-    scatter, gather, onward = {}, {}, {}
+    def took(sem, like):
+        pltpu.make_async_copy(like, like, sem).wait()
+
+    scatter, gather = {}, {}
 
     def post_scatter(o):
         for d in (1, 3, 2):
             ky, kz = (y + d) % 4, (z + d) % 4
             scatter[o, 0, d] = copy(
-                send_l.at[o, ky], left.at[o, z, y], a_s.at[0, o, d - 1], a_r.at[0, o, d - 1], at_y(d)
+                send_l.at[o, ky], left.at[o, z, y], a_s, a_r.at[0, o, d - 1], at_y(d)
             )
             scatter[o, 1, d] = copy(
-                send_r.at[o, kz], right.at[o, y, z], a_s.at[1, o, d - 1], a_r.at[1, o, d - 1], at_z(d)
+                send_r.at[o, kz], right.at[o, y, z], a_s, a_r.at[1, o, d - 1], at_z(d)
             )
 
     def post_gather(o, d):
         ky, kz = (y - d) % 4, (z - d) % 4
         for way, step in ((0, 1), (1, 3)):
-            gather[o, 0, way, d] = copy(
-                left.at[o, z, ky], left.at[o, z, ky], g_s.at[0, o, way, d], g_r.at[0, o, way, d], at_z(step)
-            )
-            gather[o, 1, way, d] = copy(
-                right.at[o, y, kz], right.at[o, y, kz], g_s.at[1, o, way, d], g_r.at[1, o, way, d], at_y(step)
-            )
+            sems = [g_r.at[side, o, d] if way == d % 2 else u_r.at[side, o] for side in range(2)]
+            gather[o, 0, way, d] = copy(left.at[o, z, ky], left.at[o, z, ky], g_s, sems[0], at_z(step))
+            gather[o, 1, way, d] = copy(right.at[o, y, kz], right.at[o, y, kz], g_s, sems[1], at_y(step))
 
     def rest_gather(o):
         for d in (1, 3, 2):
@@ -133,19 +139,13 @@
         kz, ky = (z - step) % 4, (y - step) % 4
         jy, jz = (y - d) % 4, (z - d) % 4
         gather[o, 0, way, d].wait_recv()
-        onward[o, 0, d] = copy(
-            left.at[o, kz, jy], left.at[o, kz, jy], f_s.at[0, o, d], f_r.at[0, o, d], at_z(step)
-        )
+        copy(left.at[o, kz, jy], left.at[o, kz, jy], f_s, u_r.at[0, o], at_z(step))
         gather[o, 1, way, d].wait_recv()
-        onward[o, 1, d] = copy(
-            right.at[o, ky, jz], right.at[o, ky, jz], f_s.at[1, o, d], f_r.at[1, o, d], at_y(step)
-        )
+        copy(right.at[o, ky, jz], right.at[o, ky, jz], f_s, u_r.at[1, o], at_y(step))
 
     def prepare(o):
-        for side in range(2):
-            for d in range(4):
-                gather[o, side, 1 - (d % 2), d].wait_recv()
-                onward[o, side, d].wait_recv()
+        took(u_r.at[0, o], left.at[o, 0:2])
+        took(u_r.at[1, o], right.at[o, 0:2])
         for k in range(4):
             v = left[o, k].reshape(128, 512).T
             hi = v.astype(BF16)
@@ -178,7 +178,7 @@
 
     def compute(s):
         multiply(s, 0, 1 - core)
-        exchanged[s] = copy(part.at[s, 0], part_in.at[s], d_s.at[s], d_r.at[s], sibling)
+        exchanged[s] = copy(part.at[s, 0], part_in.at[s], d_s, d_r.at[s], sibling)
         multiply(s, 1, core)
 
     up_x, down_x, far_x = (me_x + 1) % 4, (me_x + 3) % 4, (me_x + 2) % 4
@@ -188,38 +188,38 @@
         exchanged[s].wait_recv()
         part[s, 1] = part[s, 1] + part_in[s]
         mine = part.at[s, 1]
-        along_x[s, 0] = copy(mine.at[far_x, low], x_via.at[s, 0], x_s.at[s, 0], x_r.at[s, 0], at_x(1))
-        along_x[s, 1] = copy(mine.at[far_x, high], x_via.at[s, 1], x_s.at[s, 1], x_r.at[s, 1], at_x(3))
-        along_x[s, 2] = copy(mine.at[up_x, high], x_in.at[s, 0, high], x_s.at[s, 2], x_r.at[s, 2], at_x(1))
-        along_x[s, 3] = copy(mine.at[down_x, low], x_in.at[s, 1, low], x_s.at[s, 3], x_r.at[s, 3], at_x(3))
+        along_x[s, 0] = copy(mine.at[far_x, low], x_via.at[s, 0], x_s, x_r.at[s, 0], at_x(1))
+        along_x[s, 1] = copy(mine.at[far_x, high], x_via.at[s, 1], x_s, x_r.at[s, 1], at_x(3))
+        copy(mine.at[up_x, high], x_in.at[s, 0, high], x_s, x_r.at[s, 2], at_x(1))
+        copy(mine.at[down_x, low], x_in.at[s, 1, low], x_s, x_r.at[s, 2], at_x(3))
 
     def reduce_on(s):
         mine = part.at[s, 1]
         along_x[s, 0].wait_recv()
         part[s, 1, up_x, 0:128] = part[s, 1, up_x, 0:128] + x_via[s, 0]
-        along_x[s, 4] = copy(mine.at[up_x, low], x_in.at[s, 0, low], x_s.at[s, 4], x_r.at[s, 4], at_x(1))
+        copy(mine.at[up_x, low], x_in.at[s, 0, low], x_s, x_r.at[s, 2], at_x(1))
         along_x[s, 1].wait_recv()
         part[s, 1, down_x, 128:256] = part[s, 1, down_x, 128:256] + x_via[s, 1]
-        along_x[s, 5] = copy(mine.at[down_x, high], x_in.at[s, 1, high], x_s.at[s, 5], x_r.at[s, 5], at_x(3))
+        copy(mine.at[down_x, high], x_in.at[s, 1, high], x_s, x_r.at[s, 2], at_x(3))
 
     def swap(s, h, part_no):
         rows = pl.ds(pl.multiple_of(h * 128 + part_no * 64, 64), 64)
         return pltpu.make_async_remote_copy(
             dfin.at[s, rows], t_in.at[s, core, pl.ds(part_no * 64, 64)],
-            t_s.at[s, h, part_no], t_r.at[s, core, part_no], device_id=partner(h),
+            t_s.at[s], t_r.at[s], device_id=partner(h),
         )
 
     def swap_by_relay(s, h):
         rows = pl.ds(pl.multiple_of(h * 128 + 64, 64), 64)
         return pltpu.make_async_remote_copy(
-            dfin.at[s, rows], via.at[s, hop_x - 1, core], t_s.at[s, h, 1], v_r.at[s, hop_x - 1, core],
+            dfin.at[s, rows], via.at[s, hop_x - 1, core], t_s.at[s], v_r.at[s, hop_x - 1],
             device_id={"row": relay_row, "col": relay_chip * 2 + h},
         )
 
     def onto(s, k, c):
         row_s, chip_s, _ = source(k)
         return pltpu.make_async_remote_copy(
-            via.at[s, k - 1, c], t_in.at[s, c, pl.ds(64, 64)], v_s.at[s, k - 1, c], t_r.at[s, c, 1],
+            via.at[s, k - 1, c], t_in.at[s, c, pl.ds(64, 64)], v_s.at[s, k - 1], t_r.at[s],
             device_id={"row": chip_s, "col": row_s * 2 + core},
         )
 
@@ -232,16 +232,14 @@
 
             @pl.when(relays(s, k))
             def _():
+                took(v_r.at[s, k - 1], via.at[s, k - 1])
                 for c in range(2):
-                    pltpu.make_async_remote_copy(
-                        via.at[s, k - 1, c], via.at[s, k - 1, c], v_s.at[s, k - 1, c], v_r.at[s, k - 1, c], device_id=sibling
-                    ).wait_recv()
                     onto(s, k, c).start()
 
     def swap_sibling(s):
         return pltpu.make_async_remote_copy(
             dfin.at[s, pl.ds(pl.multiple_of((1 - core) * 128, 128), 128)], t_in.at[s, core],
-            t_s.at[s, 0, 0], t_r.at[s, core, 0], device_id=sibling,
+            t_s.at[s], t_r.at[s], device_id=sibling,
         )
 
     def sends(s):
@@ -250,11 +248,11 @@
     def receives(s):
         return row > colchip if s % 2 == 0 else row < colchip
 
+    written = []
     vir_b = vir[pl.ds(col, 1), :]
 
     def finish(s):
-        for k in range(2, 6):
-            along_x[s, k].wait_recv()
+        took(x_r.at[s, 2], x_in.at[s])
         p = SEQ[s][2]
         i, j = PAIRS[p]
         total = part[s, 1, me_x] + (x_in[s, 0] + x_in[s, 1])
@@ -262,6 +260,8 @@
 
         amp = total / (((occ[i] + occ[j]) - vir_a[...]) - vir_b)
         amps[p] = amp
+        written.append(pltpu.make_async_copy(amps.at[p], amps_hbm.at[p], o_s.at[p]))
+        written[-1].start()
         e_acc[p] = jnp.sum((2.0 * (amp * total)).reshape(32, 8, 128), axis=0)
 
     def swap_start(s):
@@ -288,20 +288,17 @@
     def swap_sent(s):
         @pl.when(sends(s))
         def _():
-            for h in range(2):
-                for n in range(2):
-                    swap(s, h, n).wait_send()
+            took(t_s.at[s], dfin.at[s])
 
         @pl.when(row == colchip)
         def _():
-            swap_sibling(s).wait_send()
+            took(t_s.at[s], t_in.at[s, 0])
 
         for k in range(1, 4):
 
             @pl.when(relays(s, k))
             def _():
-                for c in range(2):
-                    onto(s, k, c).wait_send()
+                took(v_s.at[s, k - 1], via.at[s, k - 1])
 
     def energy_swapped(s, weight):
         p = SEQ[s][2]
@@ -311,19 +308,12 @@
     def swapped(s):
         @pl.when(receives(s))
         def _():
-            for h in range(2):
-                for n in range(2):
-                    half = t_in.at[s, h, pl.ds(n * 64, 64)]
-                    pltpu.make_async_remote_copy(
-                        half, half, t_s.at[s, h, n], t_r.at[s, h, n], device_id=sibling
-                    ).wait_recv()
+            took(t_r.at[s], t_in.at[s])
             energy_swapped(s, 2.0)
 
         @pl.when(row == colchip)
         def _():
-            pltpu.make_async_remote_copy(
-                t_in.at[s, 1 - core], t_in.at[s, 1 - core], t_s.at[s, 0, 0], t_r.at[s, 1 - core, 0], device_id=sibling
-            ).wait_recv()
+            took(t_r.at[s], t_in.at[s, 1 - core])
             energy_swapped(s, 1.0)
 
     def forward_rest(o):
@@ -394,45 +384,44 @@
         [jnp.sum(e_acc[p], axis=0, keepdims=True) for p in range(6)] + [jnp.zeros((2, 128), F32)], axis=0
     )
     e_col[col] = e_tile
-    hops = []
     for d in range(1, 16):
-        hops.append(copy(e_col.at[col], e_col.at[col], e1_s.at[d - 1], e1_r.at[d - 1], {"col": (col + d) % 16}))
-    for cp in started[: -len(hops)]:
-        cp.wait_send()
-    del started[: -len(hops)]
+        copy(e_col.at[col], e_col.at[col], e1_s, e1_r, {"col": (col + d) % 16})
+    took(a_s, left.at[:, 0:3, 0:2])
+    took(g_s, left)
+    took(f_s, left.at[:, 0:2])
+    took(d_s, part_in)
+    took(x_s, part.at[:, 0, 0:3])
     for s in range(6):
         swap_sent(s)
-    for cp in hops:
-        cp.wait_recv()
+    took(e1_r, e_col.at[0:15])
     e_row[row] = jnp.sum(e_col[...], axis=0)
-    hops = []
     for d in range(1, 8):
-        hops.append(copy(e_row.at[row], e_row.at[row], e2_s.at[d - 1], e2_r.at[d - 1], {"row": (row + d) % 8}))
-    for cp in hops:
-        cp.wait_recv()
+        copy(e_row.at[row], e_row.at[row], e2_s, e2_r, {"row": (row + d) % 8})
+    took(e1_s, e_col.at[0:15])
+    took(e2_r, e_row.at[0:7])
     whole = jnp.sum(jnp.sum(e_row[...], axis=0), axis=1, keepdims=True)
     energy[...] = jnp.broadcast_to(whole * (2.0 / (NV * NV)), (8, 128))
-    for cp in started:
-        cp.wait_send()
+    took(e2_s, e_row.at[0:7])
+    for cp in written:
+        cp.wait()
 
 
 def local(slab, occ_energy, vir_energy):
     dma = pltpu.SemaphoreType.DMA
     vmem = pltpu.VMEM
-    both = lambda *shape: [dma(shape), dma(shape)]
     amps, energy = pl.pallas_call(
         kernel,
         out_shape=(
             jax.ShapeDtypeStruct((6, 256, 128), F32),
             jax.ShapeDtypeStruct((8, 128), F32),
         ),
-        in_specs=[
-            pl.BlockSpec(memory_space=vmem),
-            pl.BlockSpec(memory_space=pltpu.SMEM),
-            pl.BlockSpec(memory_space=vmem),
-        ],
-        out_specs=(pl.BlockSpec(memory_space=vmem), pl.BlockSpec(memory_space=vmem)),
+        in_specs=[pl.BlockSpec(memory_space=pltpu.HBM)] * 3,
+        out_specs=(pl.BlockSpec(memory_space=pltpu.HBM), pl.BlockSpec(memory_space=vmem)),
         scratch_shapes=[
+            vmem((NQ, 4, NV), F32),
+            pltpu.SMEM((4,), F32),
+            vmem((16, 128), F32),
+            vmem((6, 256, 128), F32),
             vmem((3, 4, NQ, 512), F32),
             vmem((3, 4, NQ, 512), F32),
             vmem((3, 4, 4, NQ, 512), F32),
@@ -452,18 +441,29 @@
             vmem((6, 8, 128), F32),
             vmem((16, 8, 128), F32),
             vmem((8, 8, 128), F32),
-            *both(2, 3, 3),
-            *both(2, 3, 2, 4),
-            *both(2, 3, 4),
-            *both(6),
-            *both(6, 6),
-            *both(6, 2, 2),
-            *both(6, 3, 2),
-            *both(15),
-            *both(7),
+            dma,
+            dma((2, 3, 3)),
+            dma,
+            dma((2, 3, 4)),
+            dma((2, 3)),
+            dma,
+            dma,
+            dma((6,)),
+            dma,
+            dma((6, 3)),
+            dma((6,)),
+            dma((6,)),
+            dma((6, 3)),
+            dma((6, 3)),
+            dma,
+            dma,
+            dma,
+            dma,
+            dma((3,)),
+            dma((6,)),
         ],
         compiler_params=pltpu.CompilerParams(
-            collective_id=0, has_side_effects=True, vmem_limit_bytes=48 * 2**20
+            collective_id=0, has_side_effects=True, vmem_limit_bytes=60 * 2**20
         ),
         name="pairs",
     )(slab, occ_energy, vir_energy.reshape(16, 128))

time: 100 us -> 97.1 us (0.971)
  Pallas kernels: 95.4 us -> 92.9 us
    pallas_call x1, Pallas kernels: 95.4 us -> 92.9 us  [local(): pl.pallas_call(kernel, out_shape=(jax.ShapeDtypeStruct((6, 256, 128), F32...]
    unnamed x7 -> x1, local copies, waits for them, and re-layouts: 3.45 us -> 2.06 us
where the time goes in v4:
time: 97.1 us; the launch traced here: 96.9 us
  Pallas kernels  92.9 us (96%)
  local copies, waits for them, and re-layouts  3.36 us (3%)
    pallas_call x1, Pallas kernels, local(): pl.pallas_call(kernel, out_shape=(jax.ShapeDtypeStruct((6, 256, 128), F32...  92.9 us
    unnamed x1, local copies, waits for them, and re-layouts  2.06 us

profile of v4, /device:TPU:1, one launch (start us, length us, event | category | flops | bytes accessed | tf_op | source)
XLA Modules:
  0.0 96.9 jit_solution(11565674471446977597)
XLA Ops:
  0.6 92.9 %pairs.1 = (f32[6,256,128]{2,1,0:T(8,128)}, f32[8,128]{1,0:T(8,128)}) custom-call(f32[32,4,2048]{2,1,0:T(4,128)} %slab_hbm.1, f32[4]{0:T(128)} %occ_hbm.1, f32[16,128]{1,0:T(8,128)} %bitcast.1), custom_call_target="tpu_custom_call" | custom-call | tf_op jit(solution)/shard_map/pairs/pallas_call | solution.py:412
  93.5 1.3 %slice_reduce_fusion = f32[6]{0:T(128)} fusion(f32[8,128]{1,0:T(8,128)} %get-tuple-element.5), kind=kLoop, calls=%fused_computation | loop fusion | bytes 48 | tf_op jit(solution)/shard_map/slice | solution.py:470
  94.8 2.1 %copy.6 = f32[6,256,128]{2,1,0:T(8,128)} copy(f32[6,256,128]{2,1,0:T(8,128)} %get-tuple-element.8) | data formatting | bytes 1572864

commit v5 on v4

--- a/solution.py
+++ b/solution.py
@@ -353,28 +353,31 @@
     forward_rest(2)
     swap_start(0)
     reduce_on(1)
-    reduce_on(2)
-    reduce_on(3)
     prepare(2)
     compute(4)
+    reduce_on(2)
     compute(5)
     reduce(4)
+    reduce_on(3)
     reduce(5)
-    for s in range(1, 4):
-        finish(s)
-        swap_start(s)
-        relay(s - 1)
+    relay(0)
+    finish(1)
+    swap_start(1)
+    finish(2)
     reduce_on(4)
-    swapped(0)
+    swap_start(2)
+    relay(1)
     reduce_on(5)
-    swapped(1)
+    finish(3)
+    swap_start(3)
+    relay(2)
     relay(3)
-    swapped(2)
     finish(4)
     swap_start(4)
     finish(5)
     swap_start(5)
-    swapped(3)
+    for s in range(4):
+        swapped(s)
     relay(4)
     relay(5)
     swapped(4)

time: 97.1 us -> 95.4 us (0.982)
  Pallas kernels: 92.9 us -> 91.2 us
    pallas_call x1, Pallas kernels: 92.9 us -> 91.2 us  [local(): pl.pallas_call(kernel, out_shape=(jax.ShapeDtypeStruct((6, 256, 128), F32...]
where the time goes in v5:
time: 95.4 us; the launch traced here: 95.2 us
  Pallas kernels  91.2 us (96%)
  local copies, waits for them, and re-layouts  3.36 us (4%)
    pallas_call x1, Pallas kernels, local(): pl.pallas_call(kernel, out_shape=(jax.ShapeDtypeStruct((6, 256, 128), F32...  91.2 us
    unnamed x1, local copies, waits for them, and re-layouts  2.06 us

profile of v5, /device:TPU:1, one launch (start us, length us, event | category | flops | bytes accessed | tf_op | source)
XLA Modules:
  0.0 95.2 jit_solution(7509078967049048668)
XLA Ops:
  0.6 91.2 %pairs.1 = (f32[6,256,128]{2,1,0:T(8,128)}, f32[8,128]{1,0:T(8,128)}) custom-call(f32[32,4,2048]{2,1,0:T(4,128)} %slab_hbm.1, f32[4]{0:T(128)} %occ_hbm.1, f32[16,128]{1,0:T(8,128)} %bitcast.1), custom_call_target="tpu_custom_call" | custom-call | tf_op jit(solution)/shard_map/pairs/pallas_call | solution.py:415
  91.8 1.3 %slice_reduce_fusion = f32[6]{0:T(128)} fusion(f32[8,128]{1,0:T(8,128)} %get-tuple-element.5), kind=kLoop, calls=%fused_computation | loop fusion | bytes 48 | tf_op jit(solution)/shard_map/slice | solution.py:473
  93.1 2.1 %copy.6 = f32[6,256,128]{2,1,0:T(8,128)} copy(f32[6,256,128]{2,1,0:T(8,128)} %get-tuple-element.8) | data formatting | bytes 1572864

commit v6 on v5

--- a/solution.py
+++ b/solution.py
@@ -402,8 +402,9 @@
         copy(e_row.at[row], e_row.at[row], e2_s, e2_r, {"row": (row + d) % 8})
     took(e1_s, e_col.at[0:15])
     took(e2_r, e_row.at[0:7])
-    whole = jnp.sum(jnp.sum(e_row[...], axis=0), axis=1, keepdims=True)
-    energy[...] = jnp.broadcast_to(whole * (2.0 / (NV * NV)), (8, 128))
+    whole = jnp.sum(e_row[...], axis=0)
+    for p in range(6):
+        energy[p] = jnp.sum(whole[p : p + 1]) * (2.0 / (NV * NV))
     took(e2_s, e_row.at[0:7])
     for cp in written:
         cp.wait()
@@ -416,10 +417,10 @@
         kernel,
         out_shape=(
             jax.ShapeDtypeStruct((6, 256, 128), F32),
-            jax.ShapeDtypeStruct((8, 128), F32),
+            jax.ShapeDtypeStruct((6,), F32),
         ),
         in_specs=[pl.BlockSpec(memory_space=pltpu.HBM)] * 3,
-        out_specs=(pl.BlockSpec(memory_space=pltpu.HBM), pl.BlockSpec(memory_space=vmem)),
+        out_specs=(pl.BlockSpec(memory_space=pltpu.HBM), pl.BlockSpec(memory_space=pltpu.SMEM)),
         scratch_shapes=[
             vmem((NQ, 4, NV), F32),
             pltpu.SMEM((4,), F32),
@@ -470,7 +471,7 @@
         ),
         name="pairs",
     )(slab, occ_energy, vir_energy.reshape(16, 128))
-    return amps, energy[:6, 0]
+    return amps, energy
 
 
 def solution(mesh):

time: 95.4 us -> 94.5 us (level)
    slice x1 -> x0, local copies, waits for them, and re-layouts: 1.3 us -> none  [local(): return (amps, energy[:6, 0])]
    unnamed x1 -> x4, local copies, waits for them, and re-layouts: 2.06 us -> 2.58 us
where the time goes in v6:
time: 94.5 us; the launch traced here: 94.4 us
  Pallas kernels  91.1 us (96%)
  local copies, waits for them, and re-layouts  2.58 us (3%)
    pallas_call x1, Pallas kernels, local(): pl.pallas_call(kernel, out_shape=(jax.ShapeDtypeStruct((6, 256, 128), F32...  91.1 us
    unnamed x4, local copies, waits for them, and re-layouts  2.58 us

profile of v6, /device:TPU:1, one launch (start us, length us, event | category | flops | bytes accessed | tf_op | source)
XLA Modules:
  0.0 94.4 jit_solution(13006311395956147846)
XLA Ops:
  0.6 91.1 %pairs.1 = (f32[6,256,128]{2,1,0:T(8,128)}, f32[6]{0:T(128)}) custom-call(f32[32,4,2048]{2,1,0:T(4,128)} %slab_hbm.1, f32[4]{0:T(128)} %occ_hbm.1, f32[16,128]{1,0:T(8,128)} %bitcast.1), custom_call_target="tpu_custom_call" | custom-call | tf_op jit(solution)/shard_map/pairs/pallas_call | solution.py:416
  91.8 0.0 copy-start
  91.8 2.1 %copy.7 = f32[6,256,128]{2,1,0:T(8,128)} copy(f32[6,256,128]{2,1,0:T(8,128)} %get-tuple-element.4) | data formatting | bytes 1572864
  93.8 0.0 copy-done
  93.8 0.5 copy.8
Async XLA Ops:
  91.8 2.1 %copy-start = (f32[6]{0:T(128)S(1)}, f32[6]{0:T(128)}, u32[]{:S(2)}) copy-start(f32[6]{0:T(128)} %get-tuple-element.5) | copy-start | bytes 76

commit v7 on v6

--- a/solution.py
+++ b/solution.py
@@ -326,19 +326,19 @@
     rest_gather(0)
     forward(0, 0)
     post_scatter(1)
-    post_gather(1, 0)
     stage(2)
     for h in range(2):
         vir_a[h * 128 : h * 128 + 128, :] = jnp.broadcast_to(vir[pl.ds(row * 2 + h, 1), :], (128, 128)).T
     forward_rest(0)
+    post_gather(1, 0)
     rest_gather(1)
     forward(1, 0)
     post_scatter(2)
-    post_gather(2, 0)
     prepare(0)
     compute(0)
     reduce(0)
     forward_rest(1)
+    post_gather(2, 0)
     reduce_on(0)
     rest_gather(2)
     forward(2, 0)

time: 94.5 us -> 92.6 us (0.980)
  Pallas kernels: 91.1 us -> 89.2 us
    pallas_call x1, Pallas kernels: 91.1 us -> 89.2 us  [local(): pl.pallas_call(kernel, out_shape=(jax.ShapeDtypeStruct((6, 256, 128), F32...]
where the time goes in v7:
time: 92.6 us; the launch traced here: 92.5 us
  Pallas kernels  89.2 us (96%)
  local copies, waits for them, and re-layouts  2.58 us (3%)
    pallas_call x1, Pallas kernels, local(): pl.pallas_call(kernel, out_shape=(jax.ShapeDtypeStruct((6, 256, 128), F32...  89.2 us
    unnamed x4, local copies, waits for them, and re-layouts  2.58 us

profile of v7, /device:TPU:1, one launch (start us, length us, event | category | flops | bytes accessed | tf_op | source)
XLA Modules:
  0.0 92.5 jit_solution(9864127224943875392)
XLA Ops:
  0.6 89.2 %pairs.1 = (f32[6,256,128]{2,1,0:T(8,128)}, f32[6]{0:T(128)}) custom-call(f32[32,4,2048]{2,1,0:T(4,128)} %slab_hbm.1, f32[4]{0:T(128)} %occ_hbm.1, f32[16,128]{1,0:T(8,128)} %bitcast.1), custom_call_target="tpu_custom_call" | custom-call | tf_op jit(solution)/shard_map/pairs/pallas_call | solution.py:416
  89.9 0.0 copy-start
  89.9 2.1 %copy.7 = f32[6,256,128]{2,1,0:T(8,128)} copy(f32[6,256,128]{2,1,0:T(8,128)} %get-tuple-element.4) | data formatting | bytes 1572864
  91.9 0.0 copy-done
  91.9 0.5 copy.8
Async XLA Ops:
  89.9 2.1 %copy-start = (f32[6]{0:T(128)S(1)}, f32[6]{0:T(128)}, u32[]{:S(2)}) copy-start(f32[6]{0:T(128)} %get-tuple-element.5) | copy-start | bytes 76

commit v8 on v7

--- a/solution.py
+++ b/solution.py
@@ -333,11 +333,11 @@
     post_gather(1, 0)
     rest_gather(1)
     forward(1, 0)
-    post_scatter(2)
     prepare(0)
     compute(0)
     reduce(0)
     forward_rest(1)
+    post_scatter(2)
     post_gather(2, 0)
     reduce_on(0)
     rest_gather(2)

time: 92.6 us -> 94.1 us (1.016)
  Pallas kernels: 89.2 us -> 90.7 us
    pallas_call x1, Pallas kernels: 89.2 us -> 90.7 us  [local(): pl.pallas_call(kernel, out_shape=(jax.ShapeDtypeStruct((6, 256, 128), F32...]
where the time goes in v8:
time: 94.1 us; the launch traced here: 93.9 us
  Pallas kernels  90.7 us (96%)
  local copies, waits for them, and re-layouts  2.58 us (3%)
    pallas_call x1, Pallas kernels, local(): pl.pallas_call(kernel, out_shape=(jax.ShapeDtypeStruct((6, 256, 128), F32...  90.7 us
    unnamed x4, local copies, waits for them, and re-layouts  2.58 us

profile of v8, /device:TPU:1, one launch (start us, length us, event | category | flops | bytes accessed | tf_op | source)
XLA Modules:
  0.0 93.9 jit_solution(5615255219425539157)
XLA Ops:
  0.6 90.7 %pairs.1 = (f32[6,256,128]{2,1,0:T(8,128)}, f32[6]{0:T(128)}) custom-call(f32[32,4,2048]{2,1,0:T(4,128)} %slab_hbm.1, f32[4]{0:T(128)} %occ_hbm.1, f32[16,128]{1,0:T(8,128)} %bitcast.1), custom_call_target="tpu_custom_call" | custom-call | tf_op jit(solution)/shard_map/pairs/pallas_call | solution.py:416
  91.3 0.0 copy-start
  91.3 2.1 %copy.7 = f32[6,256,128]{2,1,0:T(8,128)} copy(f32[6,256,128]{2,1,0:T(8,128)} %get-tuple-element.4) | data formatting | bytes 1572864
  93.4 0.0 copy-done
  93.4 0.5 copy.8
Async XLA Ops:
  91.3 2.1 %copy-start = (f32[6]{0:T(128)S(1)}, f32[6]{0:T(128)}, u32[]{:S(2)}) copy-start(f32[6]{0:T(128)} %get-tuple-element.5) | copy-start | bytes 76
